TPU v7x, 32 devices: a whole 2x2x4 slice. The times are simulated.
32 devices in a mesh: src: 4 (over y, x), win: 8 (over z, core).
Axes of the slice: x: 2, y: 2, z: 4, core: 2. Of those that a mesh axis runs over, the one named last changes fastest.
Arguments:
- raw: float32 [64, 262144], P('src', 'win'), may hold values from -800 to 800
- shift: int32 [64], P('src'), may hold values from 3 to 4092, as said below
- frac_bin: int32 [64], P('src'), may hold values from 0 to 63
Outputs:
- stack: float32 [2, 64, 64, 4096], P(None, 'src', None, 'win')
Inputs may be any that keep to these rules, and one draw needn't show every extreme that they name: Every node group (nodes g * 16 to g * 16 + 15) holds a node with shift exactly 4092.
All inputs are finite; a program needn't handle non-finite values.
Results may differ from a plain program's by a relative error of at most 0.0039.
Values may be sent and summed in bfloat16 or wider, within the bound.
A program may use at most 64 MiB of HBM per device.

v0:
```python
import jax
import jax.numpy as jnp
from jax import lax
from jax.sharding import PartitionSpec as P

F = 4096
N1 = 64
BAND = 128
MAXS = 4092
BINS = 64


def shifted(x, axis, by):
    count = lax.axis_size(axis)
    pairs = [(i, i + by) for i in range(count) if 0 <= i + by < count]
    return lax.ppermute(x, axis, pairs)


def broadcast(x, axis, root):
    mine = lax.axis_index(axis) == root
    return lax.psum(jnp.where(mine, x, jnp.zeros_like(x)), axis)


def tap_weights(frac_bin):
    offsets = jnp.arange(8, dtype=jnp.float32)
    spacing = offsets[None, :] - 3.0 - frac_bin.astype(jnp.float32)[:, None] / BINS
    return jnp.sinc(spacing) * jnp.sinc(spacing / 4.0)


def resample_rows(extended, shift, weights, length):

    def single_row(samples, offset, taps):
        reach = lax.dynamic_slice_in_dim(samples, offset - 3, length + 7)
        summed = jnp.zeros((length,), samples.dtype)
        for position in range(8):
            summed = summed + taps[position] * reach[position : position + length]
        return summed

    return jax.vmap(single_row)(extended, shift, weights)


def hann_window(length):
    position = jnp.arange(length, dtype=jnp.float32)
    return 0.5 - 0.5 * jnp.cos(2.0 * jnp.pi * position / length)


def whiten(real_part, imag_part):
    shape = real_part.shape
    bands = shape[-1] // BAND
    real_bands = real_part.reshape(shape[:-1] + (bands, BAND))
    imag_bands = imag_part.reshape(shape[:-1] + (bands, BAND))
    power = jnp.mean(real_bands * real_bands + imag_bands * imag_bands, axis=-1)
    denominator = jnp.sqrt(power + 1e-06)[..., None]
    return ((real_bands / denominator).reshape(shape), (imag_bands / denominator).reshape(shape))


def cosine_sine(first_count, second_count, period):
    first_index = jnp.arange(first_count, dtype=jnp.int32)[:, None]
    second_index = jnp.arange(second_count, dtype=jnp.int32)[None, :]
    cycles = first_index * second_index % period
    angle = 2.0 * jnp.pi * cycles.astype(jnp.float32) / period
    return (jnp.cos(angle), jnp.sin(angle))


def transform(segments):
    row_count = segments.shape[0]
    length = segments.shape[1]
    half = length // 2
    second = length // N1
    blocks = segments.reshape(row_count, N1, second)
    highest = lax.Precision.HIGHEST
    first_cos, first_sin = cosine_sine(N1, N1, N1)
    section_re = jnp.einsum(
        "rab,ak->rkb", blocks, first_cos, precision=highest, preferred_element_type=jnp.float32
    )
    section_im = -jnp.einsum(
        "rab,ak->rkb", blocks, first_sin, precision=highest, preferred_element_type=jnp.float32
    )
    twist_cos, twist_sin = cosine_sine(N1, second, length)
    turned_re = section_re * twist_cos + section_im * twist_sin
    turned_im = section_im * twist_cos - section_re * twist_sin
    second_cos, second_sin = cosine_sine(second, half // N1, second)
    final_re = jnp.einsum(
        "rkb,bm->rmk", turned_re, second_cos, precision=highest, preferred_element_type=jnp.float32
    ) + jnp.einsum(
        "rkb,bm->rmk", turned_im, second_sin, precision=highest, preferred_element_type=jnp.float32
    )
    final_im = jnp.einsum(
        "rkb,bm->rmk", turned_im, second_cos, precision=highest, preferred_element_type=jnp.float32
    ) - jnp.einsum(
        "rkb,bm->rmk", turned_re, second_sin, precision=highest, preferred_element_type=jnp.float32
    )
    return (final_re.reshape(row_count, half), final_im.reshape(row_count, half))


def cross_block(mine, other):
    windows_total = mine.shape[2]
    real_sum = jnp.einsum(
        "iwf,jwf->ijf", mine[0], other[0], preferred_element_type=jnp.float32
    ) + jnp.einsum("iwf,jwf->ijf", mine[1], other[1], preferred_element_type=jnp.float32)
    imag_sum = jnp.einsum(
        "iwf,jwf->ijf", mine[1], other[0], preferred_element_type=jnp.float32
    ) - jnp.einsum("iwf,jwf->ijf", mine[0], other[1], preferred_element_type=jnp.float32)
    return jnp.stack([real_sum, imag_sum]) / windows_total


def local(raw, shift, frac_bin):
    group_rows = raw.shape[0]
    local_length = raw.shape[1]
    heading = raw[:, : MAXS + 4]
    following = shifted(heading.astype(jnp.bfloat16), "win", -1).astype(heading.dtype)
    extended = jnp.concatenate([raw, following], axis=1)
    resampled = resample_rows(extended, shift, tap_weights(frac_bin), local_length)
    window_length = 2 * F
    segments = resampled.reshape(-1, window_length) * hann_window(window_length)
    real_part, imag_part = transform(segments)
    real_part = real_part.reshape(group_rows, -1, F)
    imag_part = imag_part.reshape(group_rows, -1, F)
    real_part, imag_part = (
        lax.all_to_all(real_part, "win", split_axis=2, concat_axis=1, tiled=True),
        lax.all_to_all(imag_part, "win", split_axis=2, concat_axis=1, tiled=True),
    )
    white_re, white_im = whiten(real_part, imag_part)
    white_re = white_re.astype(jnp.bfloat16)
    white_im = white_im.astype(jnp.bfloat16)
    stacked = jnp.stack([white_re, white_im])
    groups = lax.axis_size("src")
    local_freq = stacked.shape[3]
    empty = jnp.zeros((2, group_rows, group_rows * groups, local_freq), jnp.float32)

    def broadcast_step(group_index, result):
        received = broadcast(stacked, "src", group_index)
        block = cross_block(stacked, received)
        return lax.dynamic_update_slice(result, block, (0, 0, group_index * group_rows, 0))

    result = lax.fori_loop(0, groups, broadcast_step, empty)
    return result


def solution(mesh):
    return jax.shard_map(
        local,
        mesh=mesh,
        in_specs=(P("src", "win"), P("src"), P("src")),
        out_specs=P(None, "src", None, "win"),
        check_vma=False,
    )
```

profile of v0, /device:TPU:0, one launch (start us, length us, event | category | flops | bytes accessed | tf_op | source)
XLA Modules:
  0.0 789.3 jit_solution(11414815248447349638)
XLA Ops:
  10.8 3.2 pad_maximum_fusion
  13.9 78.8 %while.15 = (s32[]{:T(128)}, f32[16,36864]{1,0:T(8,128)}, s32[16,2]{0,1:T(2,128)S(1)}, f32[16,32775]{1,0:T(8,128)S(1)}, s32[]{:T(128)}, /*index=5*/s32[]{:T(128)}) while((s32[]{:T(128)}, f32[16,36864]{1,0:T(8,128)}, s32[16,2]{0,1:T(2,128)S(1)}, f32[16,32775]{1,0:T(8,128)S(1)}, s32[]{:T(128)}, /*index=5*/s32[]{:T(128)}) %tuple.58), condition=%wide.while_cond, body=%wide.while_body.sunk | while | flops 2 | bytes 524513 | solution.py:33
  14.6 2.8 dynamic-slice.7
  19.5 2.8 dynamic-slice.7
  24.4 2.8 dynamic-slice.7
  29.4 2.8 dynamic-slice.7
  34.3 2.8 dynamic-slice.7
  39.2 2.8 dynamic-slice.7
  44.1 2.8 dynamic-slice.7
  49.1 2.8 dynamic-slice.7
  54.0 2.8 dynamic-slice.7
  58.9 2.8 dynamic-slice.7
  63.9 2.8 dynamic-slice.7
  68.8 2.8 dynamic-slice.7
  73.7 2.8 dynamic-slice.7
  78.6 2.8 dynamic-slice.7
  83.6 2.8 dynamic-slice.7
  88.5 2.8 dynamic-slice.7
  92.8 4.9 multiply_add_fusion.1
  97.7 2.9 reshape.126
  100.6 3.7 fusion.11
  106.4 6.2 fusion.5
  112.6 7.6 add_bitcast_fusion.1
  122.5 6.2 copy.53
  128.7 10.1 %reshape.156 = f32[8,1,32768]{2,1,0:T(1,128)} reshape(f32[4096,4,16]{2,1,0:T(4,128)} %bitcast.148) | data formatting | bytes 2097152
  138.8 7.9 %all-to-all-start = ((f32[8,1,32768]{2,1,0:T(1,128)}), f32[8,1,32768]{2,1,0:T(1,128)S(1)}, u32[]{:S(2)}, u32[]{:S(2)}) async-start(f32[8,1,32768]{2,1,0:T(1,128)} %reshape.156), calls=%async_computation | async-start | bytes 2097152 | tf_op jit(solution)/shard_map/all_to_all | solution.py:120
  146.8 7.9 %fusion.3 = f32[64,64,64]{2,0,1:T(8,128)S(1)} fusion(f32[64,64,128]{2,0,1:T(8,128)} %copy-done.3, f32[64,64,128]{2,0,1:T(8,128)S(1)} %fusion.11, f32[64,128]{1,0:T(8,128)S(1)} %get-tuple-element.166, f32[64,128]{1,0:T(8,128)S(1)} %get-tuple-element.167), kind=kOutput, calls=%fused_computation.11 | convolution fusion | flops 404865024 | bytes 5308416 | tf_op jit(solution)/shard_map/rkb,bm->rmk/dot_general | solution.py:88
  154.7 7.6 subtract_bitcast_fusion.1
  164.6 5.9 copy.56
  170.5 10.1 %reshape.154 = f32[8,1,32768]{2,1,0:T(1,128)} reshape(f32[4096,4,16]{2,1,0:T(4,128)} %bitcast.149) | data formatting | bytes 2097152
  180.6 5.6 all-to-all-start.1
  186.7 3.0 reduce.1
  189.8 9.0 %reshape.157 = f32[4096,4,16]{2,1,0:T(4,128)} reshape(f32[8,32768]{1,0:T(8,128)S(1)} %reduce.1) | data formatting | bytes 2097152
  198.7 5.1 copy.67
  203.9 6.8 copy.68
  212.8 4.3 reduce
  217.1 9.0 %reshape.155 = f32[4096,4,16]{2,1,0:T(4,128)} reshape(f32[8,32768]{1,0:T(8,128)S(1)} %reduce) | data formatting | bytes 2097152
  226.1 6.0 copy.69
  232.1 6.7 copy.70
  250.8 4.0 copy.65
  254.8 4.7 copy.66
  261.4 5.1 copy.64
  269.0 513.5 %while.14 = (s32[]{:T(128)}, f32[2,16,64,512]{3,2,1,0:T(8,128)}, bf16[2,16,32,512]{2,1,3,0:T(8,128)(2,1)}, bf16[16,32,512]{1,0,2:T(8,128)(2,1)S(1)}, bf16[16,32,...) while((s32[]{:T(128)}, f32[2,16,64,512]{3,2,1,0:T(8,128)}, ...), condition=%wide.region_3.5_spmd, body=%wide.region_1.4_spmd.sunk | while | flops 35389448 | bytes 55050556 | solution.py:136
  269.0 4.4 broadcast_select_fusion.2
  273.4 102.9 %all-reduce.2.cloned.1.call-done = bf16[2,16,32,512]{2,1,3,0:T(8,128)(2,1)} async-done(((bf16[2,16,32,512]{2,1,3,0:T(8,128)(2,1)}), bf16[2,16,32,512]{2,1,3,0:T(8,128)(2,1)}) %all-reduce.2.cloned.1.call-update) | async-done | bytes 1048592 | tf_op jit(solution)/shard_map/while/body/eval_jaxpr/psum | solution.py:21
  376.3 3.0 fusion.148
  379.8 3.2 add_bitcast_fusion.3
  385.8 3.6 fusion.147
  389.4 3.2 subtract_bitcast_fusion.3
  398.8 106.2 %all-reduce.2.cloned.1.call-done = bf16[2,16,32,512]{2,1,3,0:T(8,128)(2,1)} async-done(((bf16[2,16,32,512]{2,1,3,0:T(8,128)(2,1)}), bf16[2,16,32,512]{2,1,3,0:T(8,128)(2,1)}) %all-reduce.2.cloned.1.call-update) | async-done | bytes 1048592 | tf_op jit(solution)/shard_map/while/body/eval_jaxpr/psum | solution.py:21
  505.0 3.0 fusion.148
  508.5 3.2 add_bitcast_fusion.3
  514.5 3.6 fusion.147
  518.1 3.2 subtract_bitcast_fusion.3
  527.5 106.1 %all-reduce.2.cloned.1.call-done = bf16[2,16,32,512]{2,1,3,0:T(8,128)(2,1)} async-done(((bf16[2,16,32,512]{2,1,3,0:T(8,128)(2,1)}), bf16[2,16,32,512]{2,1,3,0:T(8,128)(2,1)}) %all-reduce.2.cloned.1.call-update) | async-done | bytes 1048592 | tf_op jit(solution)/shard_map/while/body/eval_jaxpr/psum | solution.py:21
  633.6 3.0 fusion.148
  637.1 3.2 add_bitcast_fusion.3
  643.1 3.6 fusion.147
  646.7 3.2 subtract_bitcast_fusion.3
  656.1 106.2 %all-reduce.2.cloned.1.call-done = bf16[2,16,32,512]{2,1,3,0:T(8,128)(2,1)} async-done(((bf16[2,16,32,512]{2,1,3,0:T(8,128)(2,1)}), bf16[2,16,32,512]{2,1,3,0:T(8,128)(2,1)}) %all-reduce.2.cloned.1.call-update) | async-done | bytes 1048592 | tf_op jit(solution)/shard_map/while/body/eval_jaxpr/psum | solution.py:21
  762.3 3.0 fusion.148
  765.8 3.2 add_bitcast_fusion.3
  771.8 3.6 fusion.147
  775.4 3.2 subtract_bitcast_fusion.3
  (137 shorter events, 98.7 us)
Async XLA Ops:
  7.5 3.2 collective-permute-start
  100.6 3.7 copy-start.5
  106.4 6.2 copy-start.3
  138.8 41.8 %all-to-all-start = ((f32[8,1,32768]{2,1,0:T(1,128)}), f32[8,1,32768]{2,1,0:T(1,128)S(1)}, u32[]{:S(2)}, u32[]{:S(2)}) async-start(f32[8,1,32768]{2,1,0:T(1,128)} %reshape.156), calls=%async_computation | async-start | bytes 2097152 | tf_op jit(solution)/shard_map/all_to_all | solution.py:120
  146.8 7.9 %copy-start.4 = (f32[64,64,128]{2,0,1:T(8,128)S(1)}, f32[64,64,128]{2,0,1:T(8,128)}, u32[]{:S(2)}) copy-start(f32[64,64,128]{2,0,1:T(8,128)} %copy-done.3) | copy-start | bytes 6291460
  180.6 32.2 %all-to-all-start.1 = ((f32[8,1,32768]{2,1,0:T(1,128)}), f32[8,1,32768]{2,1,0:T(1,128)}, u32[]{:S(2)}, u32[]{:S(2)}) async-start(f32[8,1,32768]{2,1,0:T(1,128)} %reshape.154), calls=%async_computation.1 | async-start | bytes 2097152 | tf_op jit(solution)/shard_map/all_to_all | solution.py:121
  238.7 9.5 %copy-start.6 = (f32[16,4,8,512]{3,0,1,2:T(8,128)}, f32[16,4,8,512]{3,0,1,2:T(8,128)S(1)}, u32[]{:S(2)}) copy-start(f32[16,4,8,512]{3,0,1,2:T(8,128)S(1)} %copy.70) | copy-start | bytes 3145732
  269.0 107.3 %all-reduce.2.cloned.1.call-start = ((), (), s32[]{:S(2)}) async-start(), calls=%async_computation.2 | async-start | bytes 8388608 | tf_op jit(solution)/shard_map/while/body/eval_jaxpr/psum | solution.py:21
  376.3 3.0 copy-start
  376.3 3.5 copy-start.2
  385.8 3.6 copy-start.1
  396.6 108.5 %all-reduce.2.cloned.1.call-start = ((), (), s32[]{:S(2)}) async-start(), calls=%async_computation.2 | async-start | bytes 8388608 | tf_op jit(solution)/shard_map/while/body/eval_jaxpr/psum | solution.py:21
  505.0 3.0 copy-start
  505.0 3.5 copy-start.2
  514.5 3.6 copy-start.1
  525.2 108.3 %all-reduce.2.cloned.1.call-start = ((), (), s32[]{:S(2)}) async-start(), calls=%async_computation.2 | async-start | bytes 8388608 | tf_op jit(solution)/shard_map/while/body/eval_jaxpr/psum | solution.py:21
  633.6 3.0 copy-start
  633.6 3.5 copy-start.2
  643.1 3.6 copy-start.1
  653.8 108.4 %all-reduce.2.cloned.1.call-start = ((), (), s32[]{:S(2)}) async-start(), calls=%async_computation.2 | async-start | bytes 8388608 | tf_op jit(solution)/shard_map/while/body/eval_jaxpr/psum | solution.py:21
  762.3 3.0 copy-start
  762.3 3.5 copy-start.2
  771.8 3.6 copy-start.1
Sparse Core Ops, SparseCore 0:
  273.6 102.7 all-reduce.1
  400.7 104.2 all-reduce.1
  529.3 104.1 all-reduce.1
  657.6 104.6 all-reduce.1
where the time goes:
time: 795 us; the launch traced here: 789 us
  waiting for transfers between devices  424 us (53%)
  local copies, waits for them, and re-layouts  209 us (26%)
  matrix products  87.1 us (11%)
  other arithmetic  40.8 us (5%)
  starting transfers between devices  14.8 us (2%)
  between operations  13.5 us (2%)
    psum x4, waiting for transfers between devices, broadcast(): return lax.psum(jnp.where(mine, x, jnp.zeros_like(x)), axis)  421 us
    gather x64, local copies, waits for them, and re-layouts  78.5 us
    unnamed x13, local copies, waits for them, and re-layouts  38.2 us
    another operation x8, local copies, waits for them, and re-layouts, cross_block(): return jnp.stack([real_sum, imag_sum]) / windows_total  22.3 us
  transfers between devices with their start and end apart: 7, of which 6 were waited for; matrix products, arithmetic and copies ran while one was open for 8% of the time, Pallas kernels for 0%

commit v1 on v0

v1 whole, which is shorter than its diff:
```python
import functools

import jax
import jax.numpy as jnp
import ml_dtypes
import numpy as np
from jax import lax
from jax.experimental import pallas as pl
from jax.experimental.pallas import tpu as pltpu
from jax.sharding import PartitionSpec as P

F = 4096
BAND = 128
MAXS = 4092
BINS = 64
LANES = 128
ROWS = 2 * F // LANES
BANDS = F // BAND
HEAD = (MAXS + 4) // LANES
VMEM_LIMIT = 48 * 1024 * 1024


def tap_weights(frac_bin):
    offsets = jnp.arange(8, dtype=jnp.float32)
    spacing = offsets[None, :] - 3.0 - frac_bin.astype(jnp.float32)[:, None] / BINS
    return jnp.sinc(spacing) * jnp.sinc(spacing / 4.0)


def split_columns(matrix):
    high = matrix.astype(ml_dtypes.bfloat16)
    low = (matrix - high.astype(np.float64)).astype(ml_dtypes.bfloat16)
    return np.concatenate([high, high, low], axis=1)


def tables():
    r = np.arange(ROWS)
    lane = np.arange(LANES)
    band = np.arange(BANDS)
    first = 2 * np.pi * (np.outer(r, r) % ROWS) / ROWS
    first = split_columns(np.concatenate([np.cos(first), -np.sin(first)], axis=0))
    turn = 2 * np.pi * (np.outer(lane, lane) % (2 * F)) / (2 * F)
    twist = np.stack([np.cos(turn), np.sin(turn)]).astype(np.float32)
    second = 2 * np.pi * (np.outer(band, lane) % ROWS) / ROWS
    cos, sin = np.cos(second), np.sin(second)
    second = split_columns(np.block([[cos, sin], [-sin, cos]]))
    position = np.arange(2 * F).reshape(ROWS, LANES)
    hann = (0.5 - 0.5 * np.cos(2 * np.pi * position / (2 * F))).astype(np.float32)
    return first, twist, second, hann


def split_value(value):
    high = value.astype(jnp.bfloat16)
    low = (value - high.astype(jnp.float32)).astype(jnp.bfloat16)
    return high, low


def spectra_kernel(
    windows, shift_ref, taps_ref, raw_ref, next_ref, first_ref, twist_ref, second_ref, hann_ref,
    out_ref, line, white,
):
    node = pl.program_id(0)
    nodes = pl.num_programs(0)
    length = windows * ROWS
    line[0:length, :] = raw_ref[0]
    line[length : length + HEAD, :] = next_ref[0].astype(jnp.float32)
    line[length + HEAD : length + HEAD + 8, :] = jnp.zeros((8, LANES), jnp.float32)
    lane = lax.broadcasted_iota(jnp.int32, (ROWS, LANES), 1)
    columns = []
    for w in range(windows):
        total = jnp.zeros((ROWS, LANES), jnp.float32)
        for tap in range(8):
            offset = shift_ref[node] + (tap - 3)
            row, by = offset // LANES, offset % LANES
            here = line[pl.ds(row + w * ROWS, ROWS), :]
            after = line[pl.ds(row + w * ROWS + 1, ROWS), :]
            joined = jnp.where(lane >= by, here, after)
            total = total + taps_ref[node, tap] * pltpu.roll(joined, (LANES - by) % LANES, 1)
        high, low = split_value(total * hann_ref[...])
        columns.append(jnp.concatenate([high, low, high], axis=0))
    section = jnp.dot(
        first_ref[...], jnp.concatenate(columns, axis=1), preferred_element_type=jnp.float32
    )
    turned = []
    for w in range(windows):
        re = section[:ROWS, w * LANES : (w + 1) * LANES]
        im = section[ROWS:, w * LANES : (w + 1) * LANES]
        for half in range(2):
            cos = twist_ref[0, half * ROWS : (half + 1) * ROWS, :]
            sin = twist_ref[1, half * ROWS : (half + 1) * ROWS, :]
            re_high, re_low = split_value(re * cos + im * sin)
            im_high, im_low = split_value(im * cos - re * sin)
            turned.append(
                jnp.concatenate([re_high, im_high, re_low, im_low, re_high, im_high], axis=1)
            )
    final = lax.dot_general(
        second_ref[...],
        jnp.concatenate(turned, axis=0),
        (((1,), (1,)), ((), ())),
        preferred_element_type=jnp.float32,
    )
    count = out_ref.shape[4]
    for w in range(windows):
        re = final[:BANDS, w * LANES : (w + 1) * LANES]
        im = final[BANDS:, w * LANES : (w + 1) * LANES]
        power = jnp.sum(re * re + im * im, axis=-1, keepdims=True) / BAND
        scale = lax.rsqrt(power + 1e-06)
        for part, value in ((0, re), (1, im)):
            start = (part * windows + w) * BANDS * count + node
            white[pl.ds(start, BANDS, stride=count), :] = value * scale

    @pl.when(node == nodes - 1)
    def _():
        owners, owned = out_ref.shape[0], out_ref.shape[3]
        for part in range(2):
            for w in range(windows):
                start = (part * windows + w) * BANDS * count
                block = white[start : start + BANDS * count, :].astype(jnp.bfloat16)
                out_ref[:, part, w] = block.reshape(owners, owned, count, LANES)


def spectra(raw, following, shift, taps, owners):
    nodes, rows = raw.shape[:2]
    windows = rows // ROWS
    owned = BANDS // owners
    first, twist, second, hann = tables()
    shape = (owners, 2, windows, owned, nodes, LANES)
    whole = lambda array: pl.BlockSpec(array.shape, lambda i: (0,) * array.ndim)
    return pl.pallas_call(
        functools.partial(spectra_kernel, windows),
        grid=(nodes,),
        out_shape=jax.ShapeDtypeStruct(shape, jnp.bfloat16),
        in_specs=[
            pl.BlockSpec(memory_space=pltpu.SMEM),
            pl.BlockSpec(memory_space=pltpu.SMEM),
            pl.BlockSpec((1, rows, LANES), lambda i: (i, 0, 0)),
            pl.BlockSpec((1, HEAD, LANES), lambda i: (i, 0, 0)),
            whole(first),
            whole(twist),
            whole(second),
            whole(hann),
        ],
        out_specs=pl.BlockSpec(shape, lambda i: (0,) * 6),
        scratch_shapes=[
            pltpu.VMEM((rows + HEAD + 8, LANES), jnp.float32),
            pltpu.VMEM((2 * windows * BANDS * nodes, LANES), jnp.float32),
        ],
        compiler_params=pltpu.CompilerParams(vmem_limit_bytes=VMEM_LIMIT),
    )(shift, taps, raw, following, jnp.asarray(first), jnp.asarray(twist), jnp.asarray(second), jnp.asarray(hann))


def cross_group(held, read_other, write, owners, windows, owned, nodes):
    scale = 1.0 / (owners * windows)
    step = 8

    for band in range(owned):
        for chunk in range(nodes // step):

            def body(owner, sums):
                sums = list(sums)
                for w in range(windows):
                    other_re = read_other(owner, 0, w, band).astype(jnp.float32)
                    other_im = read_other(owner, 1, w, band).astype(jnp.float32)
                    other_diff = other_re - other_im
                    for k in range(step):
                        i = chunk * step + k
                        base = 3 * k
                        sums[base] += held[0, owner, w, band, i : i + 1, :] * other_re
                        sums[base + 1] += held[1, owner, w, band, i : i + 1, :] * other_im
                        sums[base + 2] += held[2, owner, w, band, i : i + 1, :] * other_diff
                return tuple(sums)

            zero = jnp.zeros((nodes, LANES), jnp.float32)
            sums = lax.fori_loop(0, owners, body, (zero,) * (3 * step))
            for k in range(step):
                p, q, r = sums[3 * k : 3 * k + 3]
                write(0, chunk * step + k, band, (p + q) * scale)
                write(1, chunk * step + k, band, (r - p + q) * scale)


def hold(held, read_own, owners, windows):

    def body(owner, carry):
        for w in range(windows):
            re = read_own(owner, 0, w).astype(jnp.float32)
            im = read_own(owner, 1, w).astype(jnp.float32)
            held[0, owner, w] = re
            held[1, owner, w] = im
            held[2, owner, w] = re + im
        return carry

    lax.fori_loop(0, owners, body, 0)


def cross_kernel(own_ref, all_ref, out_ref, held):
    owners, _, windows, owned, nodes, _ = own_ref.shape

    @pl.when(pl.program_id(0) == 0)
    def _():
        hold(held, lambda o, c, w: own_ref[o, c, w], owners, windows)

    def write(part, i, band, value):
        out_ref[part, i, :, band * LANES : (band + 1) * LANES] = value

    cross_group(
        held, lambda o, c, w, b: all_ref[0, o, c, w, b], write, owners, windows, owned, nodes
    )


def cross(own, everyone):
    owners, _, windows, owned, nodes, _ = own.shape
    groups = everyone.shape[0]
    return pl.pallas_call(
        cross_kernel,
        grid=(groups,),
        out_shape=jax.ShapeDtypeStruct((2, nodes, groups * nodes, owned * LANES), jnp.float32),
        in_specs=[
            pl.BlockSpec(own.shape, lambda g: (0,) * 6),
            pl.BlockSpec((1,) + own.shape, lambda g: (g, 0, 0, 0, 0, 0, 0)),
        ],
        out_specs=pl.BlockSpec((2, nodes, nodes, owned * LANES), lambda g: (0, 0, g, 0)),
        scratch_shapes=[pltpu.VMEM((3, owners, windows, owned, nodes, LANES), jnp.float32)],
        compiler_params=pltpu.CompilerParams(vmem_limit_bytes=VMEM_LIMIT),
    )(own, everyone)


def local(raw, shift, frac_bin):
    owners = lax.axis_size("win")
    raw = raw.reshape(raw.shape[0], -1, LANES)
    heading = raw[:, :HEAD].astype(jnp.bfloat16)
    following = lax.ppermute(heading, "win", [(i, i - 1) for i in range(1, owners)])
    white = spectra(raw, following, shift, tap_weights(frac_bin), owners)
    own = lax.all_to_all(white, "win", split_axis=0, concat_axis=0, tiled=True)
    everyone = lax.all_gather(own, "src", axis=0)
    return cross(own, everyone)


def solution(mesh):
    return jax.shard_map(
        local,
        mesh=mesh,
        in_specs=(P("src", "win"), P("src"), P("src")),
        out_specs=P(None, "src", None, "win"),
        check_vma=False,
    )
```

time: 795 us -> 146 us (0.18)
  waiting for transfers between devices: 424 us -> 53.7 us
  local copies, waits for them, and re-layouts: 209 us -> 5.57 us
  matrix products: 87.1 us -> 0 us
  other arithmetic: 40.8 us -> 0.11 us
  Pallas kernels: 0 us -> 37.4 us
  blocking collectives: 0 us -> 34.4 us
  starting transfers between devices: 14.8 us -> 1.33 us
    psum x4 -> x0, waiting for transfers between devices: 421 us -> none  [broadcast(): return lax.psum(jnp.where(mine, x, jnp.zeros_like(x)), axis)]
    dot_general x22 -> x0, matrix products: 87.1 us -> none  [the longest x4 14.4 us: cross_block(): jnp.einsum('iwf,jwf->ijf', mine[1], other[0], preferred_element_type=jnp....]
    gather x64 -> x0, local copies, waits for them, and re-layouts: 78.5 us -> none
    all_gather x0 -> x1, waiting for transfers between devices: none -> 51.8 us  [local(): everyone = lax.all_gather(own, 'src', axis=0)]
    another operation x12 -> x0, local copies, waits for them, and re-layouts: 39 us -> none  [the longest x8 22.3 us: cross_block(): return jnp.stack([real_sum, imag_sum]) / windows_total]
    pallas_call x0 -> x2, Pallas kernels: none -> 37.4 us  [the longest x1 19.2 us: cross(): pl.pallas_call(cross_kernel, grid=(groups,), out_shape=jax.ShapeDtypeStru...]
    all_to_all x0 -> x1, blocking collectives: none -> 34.4 us  [local(): own = lax.all_to_all(white, 'win', split_axis=0, concat_axis=0, tiled=True)]
    unnamed x13 -> x17, local copies, waits for them, and re-layouts: 38.2 us -> 5.55 us
  transfers between devices with their start and end apart: 7 -> 2, of which waited for: 6 -> 2; matrix products, arithmetic and copies ran while one was open for 8% -> 0% of each run, Pallas kernels for 0% -> 0%
where the time goes in v1:
time: 146 us
  waiting for transfers between devices  53.7 us (37%)
  Pallas kernels  37.4 us (26%)
  blocking collectives  34.4 us (24%)
  between operations  13.5 us (9%)
  local copies, waits for them, and re-layouts  5.57 us (4%)
    all_gather x1, waiting for transfers between devices, local(): everyone = lax.all_gather(own, 'src', axis=0)  51.8 us
    all_to_all x1, blocking collectives, local(): own = lax.all_to_all(white, 'win', split_axis=0, concat_axis=0, tiled=True)  34.4 us
    pallas_call x1, Pallas kernels, cross(): pl.pallas_call(cross_kernel, grid=(groups,), out_shape=jax.ShapeDtypeStru...  19.2 us
    pallas_call x1, Pallas kernels, spectra(): pl.pallas_call(functools.partial(spectra_kernel, windows), grid=(nodes,),...  18.1 us
    unnamed x17, local copies, waits for them, and re-layouts  5.55 us
  transfers between devices with their start and end apart: 2, of which 2 were waited for; matrix products, arithmetic and copies ran while one was open for 0% of the time, Pallas kernels for 0%

profile of v1, /device:TPU:0, one launch (start us, length us, event | category | flops | bytes accessed | tf_op | source)
XLA Modules:
  0.0 145.9 jit_solution(17960148738226272254)
XLA Ops:
  6.5 0.0 copy-start.5
  6.5 0.0 copy-start.3
  6.5 0.0 copy-start.2
  6.5 0.0 copy-start.4
  6.5 0.0 copy-start.7
  6.5 0.0 copy-start.6
  6.6 0.0 all-gather.3.cloned.1.call-start
  6.6 2.1 %copy.8 = f32[2,8,256,128]{3,2,1,0:T(8,128)S(1)} copy(f32[2,8,256,128]{3,1,2,0:T(8,128)} %bitcast.6) | data formatting | bytes 4194304
  8.7 1.3 collective-permute-start
  10.1 0.0 copy-done.7
  10.1 0.1 fusion.13.taps_ref
  10.2 1.8 %collective-permute-done.next_ref = bf16[16,32,128]{2,1,0:T(8,128)(2,1)S(1)} collective-permute-done((bf16[16,32,128]{2,1,0:T(8,128)(2,1)S(1)}, bf16[16,32,128]{2,1,0:T(8,128)(2,1)S(1)}, u32[]{:S(2)}, u32[]{:S(2)}) %collective-permute-start) | collective-permute-done | bytes 131104 | tf_op jit(solution)/shard_map/ppermute | solution.py:230
  12.0 0.0 copy-done.5
  12.0 0.0 copy-done.3
  12.0 0.0 copy-done.2
  12.0 0.0 copy-done.4
  12.0 0.0 copy-done.6
  12.0 18.1 %shard_map.73 = bf16[8,2,4,4,16,128]{5,4,3,2,1,0:T(8,128)(2,1)S(1)} custom-call(s32[16]{0:T(128)S(1)} %copy-done.6, f32[16,8]{1,0:T(8,128)S(1)} %fusion.13.taps_ref, f32[16,256,128]{2,1,0:T(8,128)S(1)} %bitcast.4, bf16[16,32,128]{2,1,0:T(8,128)(2,1)S(1)} %collective-permute-done.next_ref, bf16[128,192]{1,0:T(8,128)(2,1)S(1)} %copy-done.4, ...), custom_call_target="tpu_custom_call" | custom-call | tf_op jit(solution)/shard_map/pallas_call | solution.py:128
  30.2 34.4 %all_to_all.5.own_ref = bf16[8,2,4,4,16,128]{5,4,3,2,1,0:T(8,128)(2,1)} all-to-all(bf16[8,2,4,4,16,128]{5,4,3,2,1,0:T(8,128)(2,1)S(1)} %shard_map.73), channel_id=1, replica_groups=mesh['src'=4,'win'=8] {'win'}, dimensions={0} | all-to-all | bytes 2097152 | tf_op jit(solution)/shard_map/all_to_all | solution.py:232
  64.6 0.0 all-gather.3.cloned.1.call-update
  64.6 51.8 %all-gather.3.cloned.1.call-done = bf16[32,2,4,4,16,128]{5,4,3,2,1,0:T(8,128)(2,1)} async-done(((bf16[8,2,4,4,16,128]{5,4,3,2,1,0:T(8,128)(2,1)}), bf16[32,2,4,4,16,128]{5,4,3,2,1,0:T(8,128)(2,1)}) %all-gather.3.cloned.1.call-update) | async-done | bytes 4194320 | tf_op jit(solution)/shard_map/all_gather | solution.py:233
  116.4 0.0 copy-start
  116.4 1.2 copy-done
  117.7 0.0 copy-start.1
  117.7 2.2 %copy-done.1 = bf16[32,2,4,4,16,128]{5,4,3,2,1,0:T(8,128)(2,1)S(1)} copy-done((bf16[32,2,4,4,16,128]{5,4,3,2,1,0:T(8,128)(2,1)S(1)}, bf16[32,2,4,4,16,128]{5,4,3,2,1,0:T(8,128)(2,1)}, u32[]{:S(2)}) %copy-start.1) | copy-done | bytes 4194328
  119.9 19.2 %shard_map.74 = f32[2,16,64,512]{3,2,1,0:T(8,128)} custom-call(bf16[8,2,4,4,16,128]{5,4,3,2,1,0:T(8,128)(2,1)S(1)} %copy-done, bf16[4,8,2,4,4,16,128]{6,5,4,3,2,1,0:T(8,128)(2,1)S(1)} %bitcast.5), custom_call_target="tpu_custom_call" | custom-call | tf_op jit(solution)/shard_map/pallas_call | solution.py:212
  (3 shorter events, 0.0 us)
Async XLA Ops:
  6.5 5.5 %copy-start.5 = (f32[64,128]{1,0:T(8,128)S(1)}, f32[64,128]{1,0:T(8,128)}, u32[]{:S(2)}) copy-start(f32[64,128]{1,0:T(8,128)} %constant.46.clone.hann_ref) | copy-start | bytes 98308
  6.5 5.5 %copy-start.3 = (bf16[64,768]{1,0:T(8,128)(2,1)S(1)}, bf16[64,768]{1,0:T(8,128)(2,1)}, u32[]{:S(2)}) copy-start(bf16[64,768]{1,0:T(8,128)(2,1)} %constant.45.clone.second_ref) | copy-start | bytes 294916
  6.5 5.5 %copy-start.2 = (f32[2,128,128]{2,1,0:T(8,128)S(1)}, f32[2,128,128]{2,1,0:T(8,128)}, u32[]{:S(2)}) copy-start(f32[2,128,128]{2,1,0:T(8,128)} %constant.44.clone.twist_ref) | copy-start | bytes 393220
  6.5 5.5 %copy-start.4 = (bf16[128,192]{1,0:T(8,128)(2,1)S(1)}, bf16[128,192]{1,0:T(8,128)(2,1)}, u32[]{:S(2)}) copy-start(bf16[128,192]{1,0:T(8,128)(2,1)} %constant.43.clone.first_ref) | copy-start | bytes 147460
  6.5 3.5 %copy-start.7 = (s32[16]{0:T(128)S(1)}, s32[16]{0:T(128)}, u32[]{:S(2)}) copy-start(s32[16]{0:T(128)} %param.10) | copy-start | bytes 196
  6.5 5.5 %copy-start.6 = (s32[16]{0:T(128)S(1)}, s32[16]{0:T(128)}, u32[]{:S(2)}) copy-start(s32[16]{0:T(128)} %shift_ref.1) | copy-start | bytes 196
  6.6 109.9 %all-gather.3.cloned.1.call-start = ((), (), s32[]{:S(2)}) async-start(), calls=%async_computation.1 | async-start | bytes 5242880 | tf_op jit(solution)/shard_map/all_gather | solution.py:233
  8.7 3.2 %collective-permute-start = (bf16[16,32,128]{2,1,0:T(8,128)(2,1)S(1)}, bf16[16,32,128]{2,1,0:T(8,128)(2,1)S(1)}, u32[]{:S(2)}, u32[]{:S(2)}) collective-permute-start(bf16[16,32,128]{2,1,0:T(8,128)(2,1)S(1)} %slice.7), channel_id=1, source_target_pairs={{1,0},{2,1},{3,2},{4,3},{5,4},{6,5},{7,6},{9,8},{10,9},{11,10},{12... | collective-permute-start | bytes 393224 | tf_op jit(solution)/shard_map/ppermute | solution.py:230
  116.4 1.2 copy-start
  117.7 2.2 %copy-start.1 = (bf16[32,2,4,4,16,128]{5,4,3,2,1,0:T(8,128)(2,1)S(1)}, bf16[32,2,4,4,16,128]{5,4,3,2,1,0:T(8,128)(2,1)}, u32[]{:S(2)}) copy-start(bf16[32,2,4,4,16,128]{5,4,3,2,1,0:T(8,128)(2,1)} %all-gather.3.cloned.1.call-done) | copy-start | bytes 12582916
Sparse Core Ops, SparseCore 0:
  64.7 51.6 all-gather.2

commit v2 on v1

--- a/solution.py
+++ b/solution.py
@@ -18,6 +18,7 @@
 BANDS = F // BAND
 HEAD = (MAXS + 4) // LANES
 VMEM_LIMIT = 48 * 1024 * 1024
+MESH = pl.DeviceIdType.MESH
 
 
 def tap_weights(frac_bin):
@@ -148,79 +149,187 @@
     )(shift, taps, raw, following, jnp.asarray(first), jnp.asarray(twist), jnp.asarray(second), jnp.asarray(hann))
 
 
-def cross_group(held, read_other, write, owners, windows, owned, nodes):
+def exchange_kernel(
+    lag, white_ref, out_ref, recv, held, send_sem, recv_sem, out_sem, in_sem, own_sem
+):
+    owners, _, windows, owned, nodes, _ = white_ref.shape
+    groups = recv.shape[0]
     scale = 1.0 / (owners * windows)
     step = 8
-
-    for band in range(owned):
-        for chunk in range(nodes // step):
-
-            def body(owner, sums):
-                sums = list(sums)
+    me_w, me_g = lax.axis_index("win"), lax.axis_index("src")
+
+    def wrap(index, count):
+        return lax.rem(index + count, count)
+
+    barrier = pltpu.get_barrier_semaphore()
+    for d in range(1, owners):
+        pl.semaphore_signal(
+            barrier, inc=1, device_id={"win": wrap(me_w + d, owners)}, device_id_type=MESH
+        )
+    for e in range(1, groups):
+        pl.semaphore_signal(
+            barrier, inc=1, device_id={"src": wrap(me_g + e, groups)}, device_id_type=MESH
+        )
+    own = pltpu.make_async_copy(white_ref.at[me_w], recv.at[me_g, me_w], own_sem)
+    own.start()
+    out_ref[...] = jnp.zeros_like(out_ref)
+    pl.semaphore_wait(barrier, owners + groups - 2)
+
+    def across(d):
+        target = wrap(me_w + d, owners)
+        return pltpu.make_async_remote_copy(
+            src_ref=white_ref.at[target],
+            dst_ref=recv.at[me_g, me_w],
+            send_sem=send_sem.at[d],
+            recv_sem=recv_sem.at[d],
+            device_id={"win": target},
+            device_id_type=MESH,
+        )
+
+    def arriving(d):
+        return pltpu.make_async_remote_copy(
+            src_ref=white_ref.at[me_w],
+            dst_ref=recv.at[me_g, wrap(me_w - d, owners)],
+            send_sem=send_sem.at[d],
+            recv_sem=recv_sem.at[d],
+            device_id={"win": wrap(me_w + d, owners)},
+            device_id_type=MESH,
+        )
+
+    def forward(e, d):
+        slot = wrap(me_w - d, owners)
+        return pltpu.make_async_remote_copy(
+            src_ref=recv.at[me_g, slot],
+            dst_ref=recv.at[me_g, slot],
+            send_sem=out_sem.at[e, d],
+            recv_sem=in_sem.at[e, d],
+            device_id={"src": wrap(me_g + e, groups)},
+            device_id_type=MESH,
+        )
+
+    def forwarded(e, d):
+        slot = wrap(me_w - d, owners)
+        group = wrap(me_g - e, groups)
+        return pltpu.make_async_remote_copy(
+            src_ref=recv.at[group, slot],
+            dst_ref=recv.at[group, slot],
+            send_sem=out_sem.at[e, d],
+            recv_sem=in_sem.at[e, d],
+            device_id={"src": wrap(me_g + e, groups)},
+            device_id_type=MESH,
+        )
+
+    def hold(slot):
+        for w in range(windows):
+            re = recv[me_g, slot, 0, w].astype(jnp.float32) * scale
+            im = recv[me_g, slot, 1, w].astype(jnp.float32) * scale
+            held[0, slot, w] = re
+            held[1, slot, w] = im
+            held[2, slot, w] = re + im
+
+    def add(group, slot):
+        rows = pl.ds(pl.multiple_of(group * nodes, nodes), nodes)
+
+        def body(band, carry):
+            columns = pl.ds(pl.multiple_of(band * LANES, LANES), LANES)
+            for chunk in range(nodes // step):
+                sums = [jnp.zeros((nodes, LANES), jnp.float32)] * (3 * step)
                 for w in range(windows):
-                    other_re = read_other(owner, 0, w, band).astype(jnp.float32)
-                    other_im = read_other(owner, 1, w, band).astype(jnp.float32)
+                    other_re = recv[group, slot, 0, w, band].astype(jnp.float32)
+                    other_im = recv[group, slot, 1, w, band].astype(jnp.float32)
                     other_diff = other_re - other_im
                     for k in range(step):
                         i = chunk * step + k
-                        base = 3 * k
-                        sums[base] += held[0, owner, w, band, i : i + 1, :] * other_re
-                        sums[base + 1] += held[1, owner, w, band, i : i + 1, :] * other_im
-                        sums[base + 2] += held[2, owner, w, band, i : i + 1, :] * other_diff
-                return tuple(sums)
-
-            zero = jnp.zeros((nodes, LANES), jnp.float32)
-            sums = lax.fori_loop(0, owners, body, (zero,) * (3 * step))
-            for k in range(step):
-                p, q, r = sums[3 * k : 3 * k + 3]
-                write(0, chunk * step + k, band, (p + q) * scale)
-                write(1, chunk * step + k, band, (r - p + q) * scale)
-
-
-def hold(held, read_own, owners, windows):
-
-    def body(owner, carry):
-        for w in range(windows):
-            re = read_own(owner, 0, w).astype(jnp.float32)
-            im = read_own(owner, 1, w).astype(jnp.float32)
-            held[0, owner, w] = re
-            held[1, owner, w] = im
-            held[2, owner, w] = re + im
-        return carry
-
-    lax.fori_loop(0, owners, body, 0)
-
-
-def cross_kernel(own_ref, all_ref, out_ref, held):
-    owners, _, windows, owned, nodes, _ = own_ref.shape
-
-    @pl.when(pl.program_id(0) == 0)
-    def _():
-        hold(held, lambda o, c, w: own_ref[o, c, w], owners, windows)
-
-    def write(part, i, band, value):
-        out_ref[part, i, :, band * LANES : (band + 1) * LANES] = value
-
-    cross_group(
-        held, lambda o, c, w, b: all_ref[0, o, c, w, b], write, owners, windows, owned, nodes
-    )
-
-
-def cross(own, everyone):
-    owners, _, windows, owned, nodes, _ = own.shape
-    groups = everyone.shape[0]
+                        sums[3 * k] += held[0, slot, w, band, i : i + 1, :] * other_re
+                        sums[3 * k + 1] += held[1, slot, w, band, i : i + 1, :] * other_im
+                        sums[3 * k + 2] += held[2, slot, w, band, i : i + 1, :] * other_diff
+                for k in range(step):
+                    p, q, r = sums[3 * k : 3 * k + 3]
+                    i = chunk * step + k
+                    out_ref[0, i, rows, columns] += p + q
+                    out_ref[1, i, rows, columns] += r - p + q
+            return carry
+
+        lax.fori_loop(0, owned, body, 0)
+
+    def send(d, carry):
+        across(d).start()
+        return carry
+
+    lax.fori_loop(1, owners, send, 0)
+    own.wait()
+
+    def arrive(d):
+        for e in range(1, groups):
+            forward(e, d).start()
+        slot = wrap(me_w - d, owners)
+        hold(slot)
+        add(me_g, slot)
+
+    def finish(d):
+        slot = wrap(me_w - d, owners)
+
+        def body(e, carry):
+            forwarded(e, d).wait_recv()
+            add(wrap(me_g - e, groups), slot)
+            return carry
+
+        lax.fori_loop(1, groups, body, 0)
+
+    def first(d, carry):
+        arriving(d).wait_recv()
+        arrive(d)
+        return carry
+
+    def middle(d, carry):
+        arriving(d).wait_recv()
+        arrive(d)
+        finish(d - lag)
+        return carry
+
+    def last(d, carry):
+        finish(d)
+        return carry
+
+    arrive(0)
+    lax.fori_loop(1, lag, first, 0)
+    lax.fori_loop(lag, owners, middle, 0)
+    lax.fori_loop(owners - lag, owners, last, 0)
+
+    def sent(d, carry):
+        across(d).wait_send()
+        return carry
+
+    lax.fori_loop(1, owners, sent, 0)
+
+    def passed(d, carry):
+        for e in range(1, groups):
+            forward(e, d).wait_send()
+        return carry
+
+    lax.fori_loop(0, owners, passed, 0)
+
+
+def exchange(white, groups):
+    owners, _, windows, owned, nodes, _ = white.shape
     return pl.pallas_call(
-        cross_kernel,
-        grid=(groups,),
+        functools.partial(exchange_kernel, min(2, owners - 1)),
         out_shape=jax.ShapeDtypeStruct((2, nodes, groups * nodes, owned * LANES), jnp.float32),
-        in_specs=[
-            pl.BlockSpec(own.shape, lambda g: (0,) * 6),
-            pl.BlockSpec((1,) + own.shape, lambda g: (g, 0, 0, 0, 0, 0, 0)),
+        in_specs=[pl.BlockSpec(memory_space=pltpu.VMEM)],
+        out_specs=pl.BlockSpec(memory_space=pltpu.VMEM),
+        scratch_shapes=[
+            pltpu.VMEM((groups,) + white.shape, jnp.bfloat16),
+            pltpu.VMEM((3, owners, windows, owned, nodes, LANES), jnp.float32),
+            pltpu.SemaphoreType.DMA((owners,)),
+            pltpu.SemaphoreType.DMA((owners,)),
+            pltpu.SemaphoreType.DMA((groups, owners)),
+            pltpu.SemaphoreType.DMA((groups, owners)),
+            pltpu.SemaphoreType.DMA,
         ],
-        out_specs=pl.BlockSpec((2, nodes, nodes, owned * LANES), lambda g: (0, 0, g, 0)),
-        scratch_shapes=[pltpu.VMEM((3, owners, windows, owned, nodes, LANES), jnp.float32)],
-        compiler_params=pltpu.CompilerParams(vmem_limit_bytes=VMEM_LIMIT),
-    )(own, everyone)
+        compiler_params=pltpu.CompilerParams(
+            collective_id=0, has_side_effects=True, vmem_limit_bytes=VMEM_LIMIT
+        ),
+    )(white)
 
 
 def local(raw, shift, frac_bin):
@@ -229,9 +338,7 @@
     heading = raw[:, :HEAD].astype(jnp.bfloat16)
     following = lax.ppermute(heading, "win", [(i, i - 1) for i in range(1, owners)])
     white = spectra(raw, following, shift, tap_weights(frac_bin), owners)
-    own = lax.all_to_all(white, "win", split_axis=0, concat_axis=0, tiled=True)
-    everyone = lax.all_gather(own, "src", axis=0)
-    return cross(own, everyone)
+    return exchange(white, lax.axis_size("src"))
 
 
 def solution(mesh):

time: 146 us -> 81.9 us (0.56)
  waiting for transfers between devices: 53.7 us -> 1.81 us
  Pallas kernels: 37.4 us -> 74.3 us
  blocking collectives: 34.4 us -> 0 us
  between operations: 13.5 us -> 0.09 us
  local copies, waits for them, and re-layouts: 5.57 us -> 4.11 us
    all_gather x1 -> x0, waiting for transfers between devices: 51.8 us -> none  [local(): everyone = lax.all_gather(own, 'src', axis=0)]
    pallas_call x1, Pallas kernels: 19.2 us -> 56.1 us  [exchange(): pl.pallas_call(functools.partial(exchange_kernel, min(2, owners - 1)), ou...]
    all_to_all x1 -> x0, blocking collectives: 34.4 us -> none  [local(): own = lax.all_to_all(white, 'win', split_axis=0, concat_axis=0, tiled=True)]
    unnamed x17 -> x14, local copies, waits for them, and re-layouts: 5.55 us -> 4.09 us
  transfers between devices with their start and end apart: 2 -> 1, of which waited for: 2 -> 1; matrix products, arithmetic and copies ran while one was open for 0% -> 0% of each run, Pallas kernels for 0% -> 0%
where the time goes in v2:
time: 81.9 us; the launch traced here: 81.7 us
  Pallas kernels  74.3 us (91%)
  local copies, waits for them, and re-layouts  4.11 us (5%)
  waiting for transfers between devices  1.81 us (2%)
  starting transfers between devices  1.29 us (2%)
    pallas_call x1, Pallas kernels, exchange(): pl.pallas_call(functools.partial(exchange_kernel, min(2, owners - 1)), ou...  56.1 us
    pallas_call x1, Pallas kernels, spectra(): pl.pallas_call(functools.partial(spectra_kernel, windows), grid=(nodes,),...  18.2 us
    unnamed x14, local copies, waits for them, and re-layouts  4.09 us
    ppermute x1, waiting for transfers between devices, local(): lax.ppermute(heading, 'win', [(i, i - 1) for i in range(1, owners)])  1.81 us
  transfers between devices with their start and end apart: 1, of which 1 were waited for; matrix products, arithmetic and copies ran while one was open for 0% of the time, Pallas kernels for 0%

profile of v2, /device:TPU:0, one launch (start us, length us, event | category | flops | bytes accessed | tf_op | source)
XLA Modules:
  0.0 81.7 jit_solution(6280022288686881386)
XLA Ops:
  0.0 0.0 copy-start.3
  0.0 0.0 copy-start.1
  0.0 0.0 copy-start
  0.0 0.0 copy-start.2
  0.0 0.0 copy-start.5
  0.0 0.0 copy-start.4
  0.0 2.0 %copy.8 = f32[2,8,256,128]{3,2,1,0:T(8,128)S(1)} copy(f32[2,8,256,128]{3,1,2,0:T(8,128)} %bitcast.4) | data formatting | bytes 4194304
  2.1 1.3 %collective-permute-start = (bf16[16,32,128]{2,1,0:T(8,128)(2,1)S(1)}, bf16[16,32,128]{2,1,0:T(8,128)(2,1)S(1)}, u32[]{:S(2)}, u32[]{:S(2)}) collective-permute-start(bf16[16,32,128]{2,1,0:T(8,128)(2,1)S(1)} %slice.7), channel_id=1, source_target_pairs={{1,0},{2,1},{3,2},{4,3},{5,4},{6,5},{7,6},{9,8},{10,9},{11,10},{12... | collective-permute-start | bytes 393224 | tf_op jit(solution)/shard_map/ppermute | solution.py:339
  3.4 0.0 copy-done.5
  3.4 0.1 fusion.13.taps_ref
  3.5 1.8 %collective-permute-done.next_ref = bf16[16,32,128]{2,1,0:T(8,128)(2,1)S(1)} collective-permute-done((bf16[16,32,128]{2,1,0:T(8,128)(2,1)S(1)}, bf16[16,32,128]{2,1,0:T(8,128)(2,1)S(1)}, u32[]{:S(2)}, u32[]{:S(2)}) %collective-permute-start) | collective-permute-done | bytes 131104 | tf_op jit(solution)/shard_map/ppermute | solution.py:339
  5.3 0.0 copy-done.3
  5.3 0.0 copy-done.1
  5.4 0.0 copy-done
  5.4 0.0 copy-done.2
  5.4 0.0 copy-done.4
  5.4 18.2 %shard_map.73.white_ref = bf16[8,2,4,4,16,128]{5,4,3,2,1,0:T(8,128)(2,1)S(1)} custom-call(s32[16]{0:T(128)S(1)} %copy-done.4, f32[16,8]{1,0:T(8,128)S(1)} %fusion.13.taps_ref, f32[16,256,128]{2,1,0:T(8,128)S(1)} %bitcast.3, bf16[16,32,128]{2,1,0:T(8,128)(2,1)S(1)} %collective-permute-done.next_ref, bf16[128,192]{1,0:T(8,128)(2,1)S(1)} %copy-done.2, ...), custom_call_target="tpu_custom_call" | custom-call | tf_op jit(solution)/shard_map/pallas_call | solution.py:129
  23.6 56.1 %shard_map.74 = f32[2,16,64,512]{3,2,1,0:T(8,128)S(1)} custom-call(bf16[8,2,4,4,16,128]{5,4,3,2,1,0:T(8,128)(2,1)S(1)} %shard_map.73.white_ref), custom_call_target="tpu_custom_call" | custom-call | tf_op jit(solution)/shard_map/pallas_call | solution.py:315
  79.7 2.0 %copy.10 = f32[2,16,64,512]{3,2,1,0:T(8,128)} copy(f32[2,16,64,512]{3,2,1,0:T(8,128)S(1)} %shard_map.74) | data formatting | bytes 8388608
  (3 shorter events, 0.0 us)
Async XLA Ops:
  0.0 5.3 %copy-start.3 = (f32[64,128]{1,0:T(8,128)S(1)}, f32[64,128]{1,0:T(8,128)}, u32[]{:S(2)}) copy-start(f32[64,128]{1,0:T(8,128)} %constant.46.clone.hann_ref) | copy-start | bytes 98308
  0.0 5.3 %copy-start.1 = (bf16[64,768]{1,0:T(8,128)(2,1)S(1)}, bf16[64,768]{1,0:T(8,128)(2,1)}, u32[]{:S(2)}) copy-start(bf16[64,768]{1,0:T(8,128)(2,1)} %constant.45.clone.second_ref) | copy-start | bytes 294916
  0.0 5.3 %copy-start = (f32[2,128,128]{2,1,0:T(8,128)S(1)}, f32[2,128,128]{2,1,0:T(8,128)}, u32[]{:S(2)}) copy-start(f32[2,128,128]{2,1,0:T(8,128)} %constant.44.clone.twist_ref) | copy-start | bytes 393220
  0.0 5.4 %copy-start.2 = (bf16[128,192]{1,0:T(8,128)(2,1)S(1)}, bf16[128,192]{1,0:T(8,128)(2,1)}, u32[]{:S(2)}) copy-start(bf16[128,192]{1,0:T(8,128)(2,1)} %constant.43.clone.first_ref) | copy-start | bytes 147460
  0.0 3.4 %copy-start.5 = (s32[16]{0:T(128)S(1)}, s32[16]{0:T(128)}, u32[]{:S(2)}) copy-start(s32[16]{0:T(128)} %param.10) | copy-start | bytes 196
  0.0 5.4 %copy-start.4 = (s32[16]{0:T(128)S(1)}, s32[16]{0:T(128)}, u32[]{:S(2)}) copy-start(s32[16]{0:T(128)} %shift_ref.1) | copy-start | bytes 196
  2.1 3.2 %collective-permute-start = (bf16[16,32,128]{2,1,0:T(8,128)(2,1)S(1)}, bf16[16,32,128]{2,1,0:T(8,128)(2,1)S(1)}, u32[]{:S(2)}, u32[]{:S(2)}) collective-permute-start(bf16[16,32,128]{2,1,0:T(8,128)(2,1)S(1)} %slice.7), channel_id=1, source_target_pairs={{1,0},{2,1},{3,2},{4,3},{5,4},{6,5},{7,6},{9,8},{10,9},{11,10},{12... | collective-permute-start | bytes 393224 | tf_op jit(solution)/shard_map/ppermute | solution.py:339

commit v3 on v0

v3 whole, which is shorter than its diff:
```python
import functools

import jax
import jax.numpy as jnp
import ml_dtypes
import numpy as np
from jax import lax
from jax.experimental import pallas as pl
from jax.experimental.pallas import tpu as pltpu
from jax.sharding import PartitionSpec as P

F = 4096
BAND = 128
MAXS = 4092
BINS = 64
LANES = 128
ROWS = 2 * F // LANES
BANDS = F // BAND
HEAD = (MAXS + 4) // LANES
VMEM_LIMIT = 48 * 1024 * 1024
MESH = pl.DeviceIdType.MESH


def tap_weights(frac_bin):
    offsets = jnp.arange(8, dtype=jnp.float32)
    spacing = offsets[None, :] - 3.0 - frac_bin.astype(jnp.float32)[:, None] / BINS
    return jnp.sinc(spacing) * jnp.sinc(spacing / 4.0)


def split_columns(matrix):
    high = matrix.astype(ml_dtypes.bfloat16)
    low = (matrix - high.astype(np.float64)).astype(ml_dtypes.bfloat16)
    return np.concatenate([high, high, low], axis=1)


def tables():
    r = np.arange(ROWS)
    lane = np.arange(LANES)
    band = np.arange(BANDS)
    first = 2 * np.pi * (np.outer(r, r) % ROWS) / ROWS
    first = split_columns(np.concatenate([np.cos(first), -np.sin(first)], axis=0))
    turn = 2 * np.pi * (np.outer(lane, lane) % (2 * F)) / (2 * F)
    twist = np.stack([np.cos(turn), np.sin(turn)]).astype(np.float32)
    second = 2 * np.pi * (np.outer(band, lane) % ROWS) / ROWS
    cos, sin = np.cos(second), np.sin(second)
    second = split_columns(np.block([[cos, sin], [-sin, cos]]))
    position = np.arange(2 * F).reshape(ROWS, LANES)
    hann = (0.5 - 0.5 * np.cos(2 * np.pi * position / (2 * F))).astype(np.float32)
    return first, twist, second, hann


def split_value(value):
    high = value.astype(jnp.bfloat16)
    low = (value - high.astype(jnp.float32)).astype(jnp.bfloat16)
    return high, low


def stack_kernel(
    shift_ref, taps_ref, raw_ref, first_ref, twist_ref, second_ref, hann_ref, out_ref,
    heading, following, tail, flat, white, recv, held,
    head_sems, send_sem, recv_sem, out_sem, in_sem,
):
    windows, owners, _, owned, nodes, _ = white.shape
    groups = recv.shape[0]
    scale = 1.0 / (owners * windows)
    step = 8
    together = 4
    me_w, me_g = lax.axis_index("win"), lax.axis_index("src")

    def wrap(index, count):
        return lax.rem(index + count, count)

    def start_heading():
        return pltpu.make_async_remote_copy(
            src_ref=heading,
            dst_ref=following,
            send_sem=head_sems.at[0],
            recv_sem=head_sems.at[1],
            device_id={"win": wrap(me_w - 1, owners)},
            device_id_type=MESH,
        )

    def across(w, d):
        target = wrap(me_w + d, owners)
        return pltpu.make_async_remote_copy(
            src_ref=white.at[w, target],
            dst_ref=recv.at[me_g, w, me_w],
            send_sem=send_sem.at[w, d],
            recv_sem=recv_sem.at[w, d],
            device_id={"win": target},
            device_id_type=MESH,
        )

    def arriving(w, d):
        return pltpu.make_async_remote_copy(
            src_ref=white.at[w, me_w],
            dst_ref=recv.at[me_g, w, wrap(me_w - d, owners)],
            send_sem=send_sem.at[w, d],
            recv_sem=recv_sem.at[w, d],
            device_id={"win": wrap(me_w + d, owners)},
            device_id_type=MESH,
        )

    def forward(w, e, d, group):
        place = recv.at[group, w, wrap(me_w - d, owners)]
        return pltpu.make_async_remote_copy(
            src_ref=place,
            dst_ref=place,
            send_sem=out_sem.at[w, e, d],
            recv_sem=in_sem.at[w, e, d],
            device_id={"src": wrap(me_g + e, groups)},
            device_id_type=MESH,
        )

    def pass_on(w, d):
        for e in range(1, groups):
            forward(w, e, d, me_g).start()
        slot = wrap(me_w - d, owners)
        re = recv[me_g, w, slot, 0].astype(jnp.float32) * scale
        im = recv[me_g, w, slot, 1].astype(jnp.float32) * scale
        held[0, w, slot] = re
        held[1, w, slot] = im
        held[2, w, slot] = re + im

    def serve(w, low, high):

        def body(d, carry):
            arriving(w, d).wait_recv()
            pass_on(w, d)
            return carry

        lax.fori_loop(low, high, body, 0)

    def spectra(w, samples, base):
        lane = lax.broadcasted_iota(jnp.int32, (ROWS, LANES), 1)

        def body(index, carry):
            columns = []
            for u in range(together):
                node = index * together + u
                total = jnp.zeros((ROWS, LANES), jnp.float32)
                for tap in range(8):
                    offset = jnp.maximum(shift_ref[node], 3) + (tap - 3)
                    row, by = offset // LANES, offset % LANES
                    here = samples[node, pl.ds(row + base, ROWS), :]
                    after = samples[node, pl.ds(row + base + 1, ROWS), :]
                    joined = jnp.where(lane >= by, here, after)
                    turned = pltpu.roll(joined, (LANES - by) % LANES, 1)
                    total = total + taps_ref[node, tap] * turned
                high, low = split_value(total * hann_ref[...])
                columns.append(jnp.concatenate([high, low, high], axis=0))
            section = jnp.dot(
                first_ref[...],
                jnp.concatenate(columns, axis=1),
                preferred_element_type=jnp.float32,
            )
            twisted = []
            for u in range(together):
                re = section[:ROWS, u * LANES : (u + 1) * LANES]
                im = section[ROWS:, u * LANES : (u + 1) * LANES]
                for half in range(2):
                    cos = twist_ref[0, half * ROWS : (half + 1) * ROWS, :]
                    sin = twist_ref[1, half * ROWS : (half + 1) * ROWS, :]
                    re_high, re_low = split_value(re * cos + im * sin)
                    im_high, im_low = split_value(im * cos - re * sin)
                    twisted.append(
                        jnp.concatenate(
                            [re_high, im_high, re_low, im_low, re_high, im_high], axis=1
                        )
                    )
            final = lax.dot_general(
                second_ref[...],
                jnp.concatenate(twisted, axis=0),
                (((1,), (1,)), ((), ())),
                preferred_element_type=jnp.float32,
            )
            for u in range(together):
                re = final[:BANDS, u * LANES : (u + 1) * LANES]
                im = final[BANDS:, u * LANES : (u + 1) * LANES]
                power = jnp.sum(re * re + im * im, axis=-1, keepdims=True) / BAND
                factor = lax.rsqrt(power + 1e-06)
                for part, value in ((0, re), (1, im)):
                    start = part * BANDS * nodes + index * together + u
                    flat[pl.ds(start, BANDS, stride=nodes), :] = value * factor
            return carry

        half = nodes // together // 2
        lax.fori_loop(0, half, body, 0)
        if w > 0:
            middle = (owners + 1) // 2
            serve(w - 1, 1, middle)
        lax.fori_loop(half, nodes // together, body, 0)
        if w > 0:
            serve(w - 1, middle, owners)
        for part in range(2):
            block = flat[part * BANDS * nodes : (part + 1) * BANDS * nodes, :]
            block = block.astype(jnp.bfloat16)
            white[w, :, part] = block.reshape(owners, owned, nodes, LANES)
        recv[me_g, w, me_w] = white[w, me_w]

    def send(w):

        def body(d, carry):
            across(w, d).start()
            return carry

        lax.fori_loop(1, owners, body, 0)
        pass_on(w, 0)

    def add(group, w):
        rows = pl.ds(pl.multiple_of(group * nodes, nodes), nodes)

        def band_body(band, carry):
            columns = pl.ds(pl.multiple_of(band * LANES, LANES), LANES)
            for chunk in range(nodes // step):

                def body(slot, sums):
                    sums = list(sums)
                    other_re = recv[group, w, slot, 0, band].astype(jnp.float32)
                    other_im = recv[group, w, slot, 1, band].astype(jnp.float32)
                    other_diff = other_re - other_im
                    for k in range(step):
                        i = chunk * step + k
                        sums[3 * k] += held[0, w, slot, band, i : i + 1, :] * other_re
                        sums[3 * k + 1] += held[1, w, slot, band, i : i + 1, :] * other_im
                        sums[3 * k + 2] += held[2, w, slot, band, i : i + 1, :] * other_diff
                    return tuple(sums)

                zero = jnp.zeros((nodes, LANES), jnp.float32)
                sums = lax.fori_loop(0, owners, body, (zero,) * (3 * step), unroll=4)
                for k in range(step):
                    p, q, r = sums[3 * k : 3 * k + 3]
                    i = chunk * step + k
                    if w == 0:
                        out_ref[0, i, rows, columns] = p + q
                        out_ref[1, i, rows, columns] = r - p + q
                    else:
                        out_ref[0, i, rows, columns] += p + q
                        out_ref[1, i, rows, columns] += r - p + q
            return carry

        lax.fori_loop(0, owned, band_body, 0)

    def finish(w):

        def body(e, carry):
            group = wrap(me_g - e, groups)

            def landed(d, inner):
                forward(w, e, d, group).wait_recv()
                return inner

            lax.fori_loop(0, owners, landed, 0)
            add(group, w)
            return carry

        lax.fori_loop(1, groups, body, 0)

    barrier = pltpu.get_barrier_semaphore()
    for d in range(1, owners):
        pl.semaphore_signal(
            barrier, inc=1, device_id={"win": wrap(me_w + d, owners)}, device_id_type=MESH
        )
    for e in range(1, groups):
        pl.semaphore_signal(
            barrier, inc=1, device_id={"src": wrap(me_g + e, groups)}, device_id_type=MESH
        )
    heading[...] = raw_ref[:, :HEAD, :].astype(jnp.bfloat16)

    for w in range(windows):
        if w < windows - 1:
            spectra(w, raw_ref, w * ROWS)
        else:
            @pl.when(me_w < owners - 1)
            def _():
                start_heading().wait_recv()

            @pl.when(me_w == owners - 1)
            def _():
                following[...] = jnp.zeros_like(following)

            tail[:, :ROWS, :] = raw_ref[:, w * ROWS :, :]
            tail[:, ROWS : ROWS + HEAD, :] = following[...].astype(jnp.float32)
            tail[:, ROWS + HEAD :, :] = jnp.zeros((nodes, 8, LANES), jnp.float32)
            spectra(w, tail, 0)
        if w == 0:
            pl.semaphore_wait(barrier, owners + groups - 2)

            @pl.when(me_w > 0)
            def _():
                start_heading().start()

        send(w)
        if w >= 1:
            add(me_g, w - 1)
        if w >= 2:
            finish(w - 2)
    serve(windows - 1, 1, owners)
    if windows >= 2:
        finish(windows - 2)
    add(me_g, windows - 1)
    finish(windows - 1)

    @pl.when(me_w > 0)
    def _():
        start_heading().wait_send()

    for w in range(windows):

        def sent(d, carry):
            across(w, d).wait_send()
            return carry

        lax.fori_loop(1, owners, sent, 0)

        def passed(d, carry):
            for e in range(1, groups):
                forward(w, e, d, me_g).wait_send()
            return carry

        lax.fori_loop(0, owners, passed, 0)


def stacked(raw, shift, taps, owners, groups):
    nodes, rows = raw.shape[:2]
    windows = rows // ROWS
    owned = BANDS // owners
    chunk = (2, owned, nodes, LANES)
    constants = [jnp.asarray(table) for table in tables()]
    smem = pl.BlockSpec(memory_space=pltpu.SMEM)
    vmem = pl.BlockSpec(memory_space=pltpu.VMEM)
    return pl.pallas_call(
        stack_kernel,
        out_shape=jax.ShapeDtypeStruct((2, nodes, groups * nodes, owned * LANES), jnp.float32),
        in_specs=[smem, smem] + [vmem] * 5,
        out_specs=vmem,
        scratch_shapes=[
            pltpu.VMEM((nodes, HEAD, LANES), jnp.bfloat16),
            pltpu.VMEM((nodes, HEAD, LANES), jnp.bfloat16),
            pltpu.VMEM((nodes, ROWS + HEAD + 8, LANES), jnp.float32),
            pltpu.VMEM((2 * BANDS * nodes, LANES), jnp.float32),
            pltpu.VMEM((windows, owners) + chunk, jnp.bfloat16),
            pltpu.VMEM((groups, windows, owners) + chunk, jnp.bfloat16),
            pltpu.VMEM((3, windows, owners) + chunk[1:], jnp.float32),
            pltpu.SemaphoreType.DMA((2,)),
            pltpu.SemaphoreType.DMA((windows, owners)),
            pltpu.SemaphoreType.DMA((windows, owners)),
            pltpu.SemaphoreType.DMA((windows, groups, owners)),
            pltpu.SemaphoreType.DMA((windows, groups, owners)),
        ],
        compiler_params=pltpu.CompilerParams(
            collective_id=0, has_side_effects=True, vmem_limit_bytes=VMEM_LIMIT
        ),
    )(shift, taps, raw, *constants)


def local(raw, shift, frac_bin):
    owners = lax.axis_size("win")
    raw = raw.reshape(raw.shape[0], -1, LANES)
    return stacked(raw, shift, tap_weights(frac_bin), owners, lax.axis_size("src"))


def solution(mesh):
    return jax.shard_map(
        local,
        mesh=mesh,
        in_specs=(P("src", "win"), P("src"), P("src")),
        out_specs=P(None, "src", None, "win"),
        check_vma=False,
    )
```

time: 795 us -> 77.7 us (0.10)
  waiting for transfers between devices: 424 us -> 0 us
  local copies, waits for them, and re-layouts: 209 us -> 6.93 us
  matrix products: 87.1 us -> 0 us
  Pallas kernels: 0 us -> 69.7 us
  other arithmetic: 40.8 us -> 0.81 us
  starting transfers between devices: 14.8 us -> 0 us
  between operations: 13.5 us -> 0.06 us
    psum x4 -> x0, waiting for transfers between devices: 421 us -> none  [broadcast(): return lax.psum(jnp.where(mine, x, jnp.zeros_like(x)), axis)]
    dot_general x22 -> x0, matrix products: 87.1 us -> none  [the longest x4 14.4 us: cross_block(): jnp.einsum('iwf,jwf->ijf', mine[1], other[0], preferred_element_type=jnp....]
    gather x64 -> x0, local copies, waits for them, and re-layouts: 78.5 us -> none
    pallas_call x0 -> x1, Pallas kernels: none -> 69.7 us  [stacked(): pl.pallas_call(stack_kernel, out_shape=jax.ShapeDtypeStruct((2, nodes, gr...]
    another operation x12 -> x0, local copies, waits for them, and re-layouts: 39 us -> none  [the longest x8 22.3 us: cross_block(): return jnp.stack([real_sum, imag_sum]) / windows_total]
    unnamed x13 -> x12, local copies, waits for them, and re-layouts: 38.2 us -> 6.93 us
    all_to_all x5 -> x0, local copies, waits for them, and re-layouts: 25.1 us -> none  [the longest x3 13.2 us: local(): lax.all_to_all(imag_part, 'win', split_axis=2, concat_axis=1, tiled=True)]
    while x27 -> x0, local copies, waits for them, and re-layouts: 15.8 us -> none  [the longest x3 13.7 us: local(): result = lax.fori_loop(0, groups, broadcast_step, empty)]
  transfers between devices with their start and end apart: 7 -> 0, of which waited for: 6 -> 0; matrix products, arithmetic and copies ran while one was open for 8% -> 0% of each run, Pallas kernels for 0% -> 0%
where the time goes in v3:
time: 77.7 us; the launch traced here: 77.5 us
  Pallas kernels  69.7 us (90%)
  local copies, waits for them, and re-layouts  6.93 us (9%)
  other arithmetic  0.81 us (1%)
    pallas_call x1, Pallas kernels, stacked(): pl.pallas_call(stack_kernel, out_shape=jax.ShapeDtypeStruct((2, nodes, gr...  69.7 us
    unnamed x12, local copies, waits for them, and re-layouts  6.93 us

profile of v3, /device:TPU:0, one launch (start us, length us, event | category | flops | bytes accessed | tf_op | source)
XLA Modules:
  0.0 77.5 jit_solution(3293134845155919040)
XLA Ops:
  0.0 0.0 copy-start.3
  0.0 0.0 copy-start.1
  0.0 0.0 copy-start
  0.0 0.0 copy-start.2
  0.0 0.0 copy-start.4
  0.0 0.7 convert_multiply_fusion
  0.7 0.1 fusion.13.taps_ref
  0.8 2.0 %copy.8 = f32[2,8,256,128]{3,2,1,0:T(8,128)S(1)} copy(f32[2,8,256,128]{3,1,2,0:T(8,128)} %bitcast.3) | data formatting | bytes 4194304
  2.8 0.0 copy-done.3
  2.8 0.0 copy-done.1
  2.9 0.0 copy-done
  2.9 0.0 copy-done.2
  2.9 0.0 copy-done.4
  2.9 69.7 %shard_map.73 = f32[2,16,64,512]{3,2,1,0:T(8,128)} custom-call(s32[16]{0:T(128)S(1)} %copy-done.4, f32[16,8]{1,0:T(8,128)S(1)} %fusion.13.taps_ref, f32[16,256,128]{2,1,0:T(8,128)S(1)} %bitcast.2, bf16[128,192]{1,0:T(8,128)(2,1)S(1)} %copy-done.2, f32[2,128,128]{2,1,0:T(8,128)S(1)} %copy-done, bf16[64,768]{1,0:T(8,128)(2,1)S(1)} %copy-done.1, ...), custom_call_target="tpu_custom_call" | custom-call | tf_op jit(solution)/shard_map/pallas_call | solution.py:332
  72.5 4.9 %copy.10 = f32[2,16,64,512]{3,2,1,0:T(8,128)} copy(f32[2,16,64,512]{3,2,1,0:T(8,128)} %shard_map.73) | data formatting | bytes 8388608
  (1 shorter events, 0.0 us)
Async XLA Ops:
  0.0 2.8 %copy-start.3 = (f32[64,128]{1,0:T(8,128)S(1)}, f32[64,128]{1,0:T(8,128)}, u32[]{:S(2)}) copy-start(f32[64,128]{1,0:T(8,128)} %constant.46.clone.hann_ref) | copy-start | bytes 98308
  0.0 2.8 %copy-start.1 = (bf16[64,768]{1,0:T(8,128)(2,1)S(1)}, bf16[64,768]{1,0:T(8,128)(2,1)}, u32[]{:S(2)}) copy-start(bf16[64,768]{1,0:T(8,128)(2,1)} %constant.45.clone.second_ref) | copy-start | bytes 294916
  0.0 2.8 %copy-start = (f32[2,128,128]{2,1,0:T(8,128)S(1)}, f32[2,128,128]{2,1,0:T(8,128)}, u32[]{:S(2)}) copy-start(f32[2,128,128]{2,1,0:T(8,128)} %constant.44.clone.twist_ref) | copy-start | bytes 393220
  0.0 2.9 %copy-start.2 = (bf16[128,192]{1,0:T(8,128)(2,1)S(1)}, bf16[128,192]{1,0:T(8,128)(2,1)}, u32[]{:S(2)}) copy-start(bf16[128,192]{1,0:T(8,128)(2,1)} %constant.43.clone.first_ref) | copy-start | bytes 147460
  0.0 2.9 %copy-start.4 = (s32[16]{0:T(128)S(1)}, s32[16]{0:T(128)}, u32[]{:S(2)}) copy-start(s32[16]{0:T(128)} %shift_ref.1) | copy-start | bytes 196

commit v4 on v3

--- a/solution.py
+++ b/solution.py
@@ -17,7 +17,7 @@
 ROWS = 2 * F // LANES
 BANDS = F // BAND
 HEAD = (MAXS + 4) // LANES
-VMEM_LIMIT = 48 * 1024 * 1024
+VMEM_LIMIT = 32 * 1024 * 1024
 MESH = pl.DeviceIdType.MESH
 
 
@@ -101,6 +101,25 @@
             device_id_type=MESH,
         )
 
+    square = groups == 4
+    beside = me_g + 1 - 2 * lax.rem(me_g, 2)
+    above = lax.rem(me_g + 2, 4)
+    corner = 3 - me_g
+
+    def target_of(e):
+        return wrap(me_g + e, groups) if not square else (beside if e == 1 else above)
+
+    def relay(w, e, d, group, part):
+        place = recv.at[group, w, wrap(me_w - d, owners), part]
+        return pltpu.make_async_remote_copy(
+            src_ref=place,
+            dst_ref=place,
+            send_sem=out_sem.at[w, e, d],
+            recv_sem=in_sem.at[w, e, d],
+            device_id={"src": above if part == 0 else beside},
+            device_id_type=MESH,
+        )
+
     def forward(w, e, d, group):
         place = recv.at[group, w, wrap(me_w - d, owners)]
         return pltpu.make_async_remote_copy(
@@ -108,12 +127,14 @@
             dst_ref=place,
             send_sem=out_sem.at[w, e, d],
             recv_sem=in_sem.at[w, e, d],
-            device_id={"src": wrap(me_g + e, groups)},
+            device_id={"src": target_of(e)},
             device_id_type=MESH,
         )
 
+    direct = range(1, 3) if square else range(1, groups)
+
     def pass_on(w, d):
-        for e in range(1, groups):
+        for e in direct:
             forward(w, e, d, me_g).start()
         slot = wrap(me_w - d, owners)
         re = recv[me_g, w, slot, 0].astype(jnp.float32) * scale
@@ -241,7 +262,32 @@
 
         lax.fori_loop(0, owned, band_body, 0)
 
+    def finish_corner(w):
+
+        def landed(d, carry):
+            relay(w, 3, d, corner, 0).wait_recv()
+            relay(w, 0, d, corner, 1).wait_recv()
+            return carry
+
+        lax.fori_loop(0, owners, landed, 0)
+        add(corner, w)
+
     def finish(w):
+        if square:
+
+            def landed(d, carry):
+                forward(w, 1, d, beside).wait_recv()
+                relay(w, 3, d, beside, 0).start()
+                forward(w, 2, d, above).wait_recv()
+                relay(w, 0, d, above, 1).start()
+                return carry
+
+            lax.fori_loop(0, owners, landed, 0)
+            if w >= 1:
+                finish_corner(w - 1)
+            add(beside, w)
+            add(above, w)
+            return
 
         def body(e, carry):
             group = wrap(me_g - e, groups)
@@ -300,6 +346,8 @@
         finish(windows - 2)
     add(me_g, windows - 1)
     finish(windows - 1)
+    if square:
+        finish_corner(windows - 1)
 
     @pl.when(me_w > 0)
     def _():
@@ -314,8 +362,11 @@
         lax.fori_loop(1, owners, sent, 0)
 
         def passed(d, carry):
-            for e in range(1, groups):
+            for e in direct:
                 forward(w, e, d, me_g).wait_send()
+            if square:
+                relay(w, 3, d, beside, 0).wait_send()
+                relay(w, 0, d, above, 1).wait_send()
             return carry
 
         lax.fori_loop(0, owners, passed, 0)

time: 77.7 us -> 64.2 us (0.83)
  Pallas kernels: 69.7 us -> 59.1 us
  local copies, waits for them, and re-layouts: 6.93 us -> 4.03 us
    pallas_call x1, Pallas kernels: 69.7 us -> 59.1 us  [stacked(): pl.pallas_call(stack_kernel, out_shape=jax.ShapeDtypeStruct((2, nodes, gr...]
    unnamed x12, local copies, waits for them, and re-layouts: 6.93 us -> 4.03 us
where the time goes in v4:
time: 64.2 us; the launch traced here: 64 us
  Pallas kernels  59.1 us (92%)
  local copies, waits for them, and re-layouts  4.03 us (6%)
  other arithmetic  0.81 us (1%)
    pallas_call x1, Pallas kernels, stacked(): pl.pallas_call(stack_kernel, out_shape=jax.ShapeDtypeStruct((2, nodes, gr...  59.1 us
    unnamed x12, local copies, waits for them, and re-layouts  4.03 us

profile of v4, /device:TPU:0, one launch (start us, length us, event | category | flops | bytes accessed | tf_op | source)
XLA Modules:
  0.0 64.0 jit_solution(5722187278481461500)
XLA Ops:
  0.0 0.0 copy-start.3
  0.0 0.0 copy-start.1
  0.0 0.0 copy-start
  0.0 0.0 copy-start.2
  0.0 0.0 copy-start.4
  0.0 0.7 %convert_multiply_fusion = f32[16]{0:T(128)S(1)} fusion(s32[16]{0:T(128)} %param.10), kind=kLoop, calls=%fused_computation.57 | loop fusion | flops 32 | bytes 128 | tf_op jit(solution)/shard_map/div | solution.py:26
  0.7 0.1 fusion.13.taps_ref
  0.8 2.0 %copy.8 = f32[2,8,256,128]{3,2,1,0:T(8,128)S(1)} copy(f32[2,8,256,128]{3,1,2,0:T(8,128)} %bitcast.3) | data formatting | bytes 4194304
  2.8 0.0 copy-done.3
  2.8 0.0 copy-done.1
  2.9 0.0 copy-done
  2.9 0.0 copy-done.2
  2.9 0.0 copy-done.4
  2.9 59.1 %shard_map.73 = f32[2,16,64,512]{3,2,1,0:T(8,128)S(1)} custom-call(s32[16]{0:T(128)S(1)} %copy-done.4, f32[16,8]{1,0:T(8,128)S(1)} %fusion.13.taps_ref, f32[16,256,128]{2,1,0:T(8,128)S(1)} %bitcast.2, bf16[128,192]{1,0:T(8,128)(2,1)S(1)} %copy-done.2, f32[2,128,128]{2,1,0:T(8,128)S(1)} %copy-done, bf16[64,768]{1,0:T(8,128)(2,1)S(1)} %copy-done.1, ...), custom_call_target="tpu_custom_call" | custom-call | tf_op jit(solution)/shard_map/pallas_call | solution.py:383
  62.0 2.0 %copy.10 = f32[2,16,64,512]{3,2,1,0:T(8,128)} copy(f32[2,16,64,512]{3,2,1,0:T(8,128)S(1)} %shard_map.73) | data formatting | bytes 8388608
  (1 shorter events, 0.0 us)
Async XLA Ops:
  0.0 2.8 %copy-start.3 = (f32[64,128]{1,0:T(8,128)S(1)}, f32[64,128]{1,0:T(8,128)}, u32[]{:S(2)}) copy-start(f32[64,128]{1,0:T(8,128)} %constant.46.clone.hann_ref) | copy-start | bytes 98308
  0.0 2.8 %copy-start.1 = (bf16[64,768]{1,0:T(8,128)(2,1)S(1)}, bf16[64,768]{1,0:T(8,128)(2,1)}, u32[]{:S(2)}) copy-start(bf16[64,768]{1,0:T(8,128)(2,1)} %constant.45.clone.second_ref) | copy-start | bytes 294916
  0.0 2.8 %copy-start = (f32[2,128,128]{2,1,0:T(8,128)S(1)}, f32[2,128,128]{2,1,0:T(8,128)}, u32[]{:S(2)}) copy-start(f32[2,128,128]{2,1,0:T(8,128)} %constant.44.clone.twist_ref) | copy-start | bytes 393220
  0.0 2.9 %copy-start.2 = (bf16[128,192]{1,0:T(8,128)(2,1)S(1)}, bf16[128,192]{1,0:T(8,128)(2,1)}, u32[]{:S(2)}) copy-start(bf16[128,192]{1,0:T(8,128)(2,1)} %constant.43.clone.first_ref) | copy-start | bytes 147460
  0.0 2.9 %copy-start.4 = (s32[16]{0:T(128)S(1)}, s32[16]{0:T(128)}, u32[]{:S(2)}) copy-start(s32[16]{0:T(128)} %shift_ref.1) | copy-start | bytes 196
